TPU v7x, 32 devices: a whole 2x2x4 slice. The times are simulated.
32 devices in a mesh: group: 2 (over x), ctx: 8 (over z, y), head: 2 (over core).
Axes of the slice: x: 2, y: 2, z: 4, core: 2. Of those that a mesh axis runs over, the one named last changes fastest.
Arguments:
- x_in: bfloat16 [8192, 4096], P(('group', 'ctx'), 'head'), parts along dimension 0, may hold values from -0.625 to 0.625
- b_in: bfloat16 [8192, 128], P(('group', 'ctx')), parts along dimension 0, may hold values from -0.5 to 0.5
- c_in: bfloat16 [8192, 128], P(('group', 'ctx')), parts along dimension 0, may hold values from -0.5 to 0.5
- loga: float32 [8192, 64], P(('group', 'ctx'), 'head'), parts along dimension 0, may hold values from -0.8 to 0, as said below
- dout: bfloat16 [8192, 2048], P(('group', 'ctx')), parts along dimension 0, may hold values from -0.09375 to 0.09375
- w_out: bfloat16 [2048, 4096], P(None, 'head'), may hold values from -0.09375 to 0.09375
Outputs:
- grad_x: bfloat16 [8192, 4096], P(('group', 'ctx'), 'head'), parts along dimension 0
- grad_b: float32 [8192, 128], P(('group', 'ctx')), parts along dimension 0
- grad_c: float32 [8192, 128], P(('group', 'ctx')), parts along dimension 0
- grad_loga: float32 [8192, 64], P(('group', 'ctx'), 'head'), parts along dimension 0
- weight_grad: float32 [4096, 4096], P(('group', 'ctx'), 'head'), parts along dimension 0
There are 2 independent parts, one for each index of `group`. A program takes and returns all parts, laid end to end along the dimension named above; an argument that names none is the same for every part. Nothing has to cross between parts.
Inputs may be any that keep to these rules, and one draw needn't show every extreme that they name: `loga`: log decays of each step and head; negative.
All inputs are finite; a program needn't handle non-finite values.
Results may differ from a plain program's by a relative error of at most 0.017.
Values may be sent and summed in bfloat16 or wider, within the bound.
No kernel may reach another device: no remote copies, remote signals or barrier semaphores. Data moves between devices by JAX's collectives and lax.ppermute only.
A program may use at most 128 MiB of HBM per device.

v0:
```python
import jax
import jax.numpy as jnp
from jax import lax
from jax.sharding import PartitionSpec as P

STRETCH = 256


masked_out = -1e30
highest = lax.Precision.HIGHEST


def from_behind(x, axis, by):
    length = lax.axis_size(axis)
    pairs = [(i, i + by) for i in range(length) if 0 <= i + by < length]
    return lax.ppermute(x, axis, pairs)


def block_forward(state, x_block, input_matrix_tile, c_block, l_block):
    cum = jnp.cumsum(l_block, axis=0)
    count = x_block.shape[0]
    order = jnp.arange(count)
    lower = order[:, None] >= order[None, :]
    cum_t = cum.T
    diff = cum_t[:, :, None] - cum_t[:, None, :]
    decay = jnp.exp(jnp.where(lower[None, :, :], diff, masked_out))
    scores = jnp.dot(c_block, input_matrix_tile.T, precision=highest)
    weights = decay * scores[None, :, :]
    inside = jnp.einsum("hij,jhp->ihp", weights, x_block, precision=highest)
    lead = jnp.exp(cum)
    carried = jnp.einsum("in,nhp->ihp", c_block, state, precision=highest) * lead[:, :, None]
    tail = jnp.exp(cum[-1][None, :] - cum)
    fresh = jnp.einsum(
        "jn,jhp->nhp", input_matrix_tile, x_block * tail[:, :, None], precision=highest
    )
    next_state = state * jnp.exp(cum[-1])[None, :, None] + fresh
    return (next_state, inside + carried)


def local_forward(x_value, b_value, c_value, l_value, start_state):
    row_count, head_count, head_width = x_value.shape
    blocks = row_count // STRETCH
    x_blocks = x_value.reshape(blocks, STRETCH, head_count, head_width)
    b_blocks = b_value.reshape(blocks, STRETCH, b_value.shape[1])
    c_blocks = c_value.reshape(blocks, STRETCH, c_value.shape[1])
    l_blocks = l_value.reshape(blocks, STRETCH, head_count)
    stepper = jax.checkpoint(block_forward)

    def advance(state, pieces):
        return stepper(state, pieces[0], pieces[1], pieces[2], pieces[3])

    final, outputs = lax.scan(advance, start_state, (x_blocks, b_blocks, c_blocks, l_blocks))
    return (outputs.reshape(row_count, head_count, head_width), final)


def spread_decay(decay, state):
    head_width = state.shape[1] // decay.shape[0]
    return jnp.repeat(decay, head_width)[None, :]


def on_device(x_in, b_in, c_in, loga, dout, w_out):
    row_count, width = x_in.shape
    head_count = loga.shape[1]
    head_width = width // head_count
    state_count = b_in.shape[1]
    x_float = x_in.astype(jnp.float32).reshape(row_count, head_count, head_width)
    b_float = b_in.astype(jnp.float32)
    c_float = c_in.astype(jnp.float32)
    grad_y = jnp.dot(dout, w_out, preferred_element_type=jnp.float32).reshape(
        row_count, head_count, head_width
    )
    cum = jnp.cumsum(loga, axis=0)
    total = cum[-1]
    span_decay = jnp.exp(total)
    tail = jnp.exp(total[None, :] - cum)
    lead = jnp.exp(cum)
    own_state = jnp.einsum(
        "tn,thp->nhp", b_float, x_float * tail[:, :, None], precision=highest
    ).reshape(state_count, width)
    local_adjoint = jnp.einsum(
        "tn,thp->nhp", c_float, grad_y * lead[:, :, None], precision=highest
    ).reshape(state_count, width)
    column_decay = spread_decay(span_decay, own_state)
    empty = jnp.zeros((state_count, width), jnp.float32)

    def forward_turn(turn, incoming):
        outgoing = column_decay * incoming + own_state
        return from_behind(outgoing.astype(jnp.bfloat16), "ctx", 1).astype(outgoing.dtype)

    def backward_turn(turn, incoming):
        outgoing = local_adjoint + column_decay * incoming
        return from_behind(outgoing.astype(jnp.bfloat16), "ctx", -1).astype(outgoing.dtype)

    entering = lax.fori_loop(0, lax.axis_size("ctx") - 1, forward_turn, empty)
    leaving = lax.fori_loop(0, lax.axis_size("ctx") - 1, backward_turn, empty)
    start_state = entering.reshape(state_count, head_count, head_width)
    end_cotangent = leaving.reshape(state_count, head_count, head_width)

    def forward_both(x_value, b_value, c_value, l_value):
        return local_forward(x_value, b_value, c_value, l_value, start_state)

    primal, pull = jax.vjp(forward_both, x_float, b_float, c_float, loga)
    grad_x32, part_b, part_c, grad_loga = pull((grad_y, end_cotangent))
    y_half = primal[0].reshape(row_count, width).astype(jnp.bfloat16)
    weight_grad = lax.psum_scatter(
        lax.dot_general(
            dout, y_half, (((0,), (0,)), ((), ())), preferred_element_type=jnp.float32
        ).astype(jnp.bfloat16),
        "ctx",
        scatter_dimension=0,
        tiled=True,
    ).astype(jnp.float32)
    grad_b, grad_c = (
        lax.psum(part_b.astype(jnp.bfloat16), "head").astype(jnp.float32),
        lax.psum(part_c.astype(jnp.bfloat16), "head").astype(jnp.float32),
    )
    grad_x = grad_x32.reshape(row_count, width).astype(jnp.bfloat16)
    return (grad_x, grad_b, grad_c, grad_loga, weight_grad)


def solution(mesh):
    placed = (
        P(("group", "ctx"), "head"),
        P(("group", "ctx"), None),
        P(("group", "ctx"), None),
        P(("group", "ctx"), "head"),
        P(("group", "ctx"), None),
        P(None, "head"),
    )
    return jax.shard_map(
        on_device,
        mesh=mesh,
        in_specs=placed,
        out_specs=(
            P(("group", "ctx"), "head"),
            P(("group", "ctx"), None),
            P(("group", "ctx"), None),
            P(("group", "ctx"), "head"),
            P(("group", "ctx"), "head"),
        ),
        check_vma=False,
    )
```

profile of v0, /device:TPU:0, one launch (start us, length us, event | category | flops | bytes accessed | tf_op | source)
XLA Modules:
  0.0 700.3 jit_solution(6873523127774278365)
XLA Ops:
  16.0 5.5 reshape_reshape.6
  26.5 11.6 %fusion.82 = f32[512,2048]{0,1:T(8,128)} fusion(bf16[512,2048]{1,0:T(8,128)(2,1)S(1)} %copy-done, bf16[2048,2048]{1,0:T(8,128)(2,1)} %param.19), kind=kOutput, calls=%fused_computation.127 | convolution fusion | flops 4294967296 | bytes 14680064 | tf_op jit(solution)/shard_map/dot_general | solution.py:69
  38.0 5.9 reshape_reshape.7
  51.7 132.3 %while.62 = (s32[]{:T(128)}, f32[128,2048]{1,0:T(8,128)}, f32[128,2048]{1,0:T(8,128)}, f32[32]{0:T(128)S(1)}, s32[]{:T(128)}, /*index=5*/s32[]{:T(128)}) while((s32[]{:T(128)}, f32[128,2048]{1,0:T(8,128)}, f32[128,2048]{1,0:T(8,128)}, f32[32]{0:T(128)S(1)}, s32[]{:T(128)}, /*index=5*/s32[]{:T(128)}) %tuple.156), condition=%wide.region_3.4_spmd.clone, body=%wide.region_2.3_spmd.clone.sunk | while | flops 1310723 | bytes 6324471 | solution.py:95
  55.3 15.8 %collective-permute-done = bf16[128,2048]{1,0:T(8,128)(2,1)} collective-permute-done((bf16[128,2048]{1,0:T(8,128)(2,1)}, bf16[128,2048]{1,0:T(8,128)(2,1)}, u32[]{:S(2)}, u32[]{:S(2)}) %collective-permute-start) | collective-permute-done | bytes 524320 | tf_op jit(solution)/shard_map/while/body/eval_jaxpr/ppermute | solution.py:16
  77.1 14.6 %collective-permute-done = bf16[128,2048]{1,0:T(8,128)(2,1)} collective-permute-done((bf16[128,2048]{1,0:T(8,128)(2,1)}, bf16[128,2048]{1,0:T(8,128)(2,1)}, u32[]{:S(2)}, u32[]{:S(2)}) %collective-permute-start) | collective-permute-done | bytes 524320 | tf_op jit(solution)/shard_map/while/body/eval_jaxpr/ppermute | solution.py:16
  97.8 13.7 %collective-permute-done = bf16[128,2048]{1,0:T(8,128)(2,1)} collective-permute-done((bf16[128,2048]{1,0:T(8,128)(2,1)}, bf16[128,2048]{1,0:T(8,128)(2,1)}, u32[]{:S(2)}, u32[]{:S(2)}) %collective-permute-start) | collective-permute-done | bytes 524320 | tf_op jit(solution)/shard_map/while/body/eval_jaxpr/ppermute | solution.py:16
  117.5 12.8 %collective-permute-done = bf16[128,2048]{1,0:T(8,128)(2,1)} collective-permute-done((bf16[128,2048]{1,0:T(8,128)(2,1)}, bf16[128,2048]{1,0:T(8,128)(2,1)}, u32[]{:S(2)}, u32[]{:S(2)}) %collective-permute-start) | collective-permute-done | bytes 524320 | tf_op jit(solution)/shard_map/while/body/eval_jaxpr/ppermute | solution.py:16
  136.3 11.8 %collective-permute-done = bf16[128,2048]{1,0:T(8,128)(2,1)} collective-permute-done((bf16[128,2048]{1,0:T(8,128)(2,1)}, bf16[128,2048]{1,0:T(8,128)(2,1)}, u32[]{:S(2)}, u32[]{:S(2)}) %collective-permute-start) | collective-permute-done | bytes 524320 | tf_op jit(solution)/shard_map/while/body/eval_jaxpr/ppermute | solution.py:16
  154.1 10.9 %collective-permute-done = bf16[128,2048]{1,0:T(8,128)(2,1)} collective-permute-done((bf16[128,2048]{1,0:T(8,128)(2,1)}, bf16[128,2048]{1,0:T(8,128)(2,1)}, u32[]{:S(2)}, u32[]{:S(2)}) %collective-permute-start) | collective-permute-done | bytes 524320 | tf_op jit(solution)/shard_map/while/body/eval_jaxpr/ppermute | solution.py:16
  171.1 10.8 %collective-permute-done = bf16[128,2048]{1,0:T(8,128)(2,1)} collective-permute-done((bf16[128,2048]{1,0:T(8,128)(2,1)}, bf16[128,2048]{1,0:T(8,128)(2,1)}, u32[]{:S(2)}, u32[]{:S(2)}) %collective-permute-start) | collective-permute-done | bytes 524320 | tf_op jit(solution)/shard_map/while/body/eval_jaxpr/ppermute | solution.py:16
  197.1 120.5 %while.63 = (s32[]{:T(128)}, f32[128,2048]{1,0:T(8,128)S(1)}, f32[128,2048]{1,0:T(8,128)}, f32[32]{0:T(128)S(1)}, s32[]{:T(128)}, /*index=5*/s32[]{:T(128)}) while((s32[]{:T(128)}, f32[128,2048]{1,0:T(8,128)S(1)}, f32[128,2048]{1,0:T(8,128)}, f32[32]{0:T(128)S(1)}, s32[]{:T(128)}, /*index=5*/s32[]{:T(128)}) %tuple.180), condition=%wide.region_5.6_spmd.clone, body=%wide.region_4.5_spmd.clone.sunk | while | flops 1310723 | bytes 6324471 | solution.py:94
  199.4 5.7 collective-permute-start.1
  205.1 6.2 collective-permute-done.1
  219.9 7.1 %collective-permute-done.1 = bf16[128,2048]{1,0:T(8,128)(2,1)} collective-permute-done((bf16[128,2048]{1,0:T(8,128)(2,1)}, bf16[128,2048]{1,0:T(8,128)(2,1)}, u32[]{:S(2)}, u32[]{:S(2)}) %collective-permute-start.1) | collective-permute-done | bytes 524320 | tf_op jit(solution)/shard_map/while/body/eval_jaxpr/ppermute | solution.py:16
  235.8 8.2 %collective-permute-done.1 = bf16[128,2048]{1,0:T(8,128)(2,1)} collective-permute-done((bf16[128,2048]{1,0:T(8,128)(2,1)}, bf16[128,2048]{1,0:T(8,128)(2,1)}, u32[]{:S(2)}, u32[]{:S(2)}) %collective-permute-start.1) | collective-permute-done | bytes 524320 | tf_op jit(solution)/shard_map/while/body/eval_jaxpr/ppermute | solution.py:16
  252.7 9.3 %collective-permute-done.1 = bf16[128,2048]{1,0:T(8,128)(2,1)} collective-permute-done((bf16[128,2048]{1,0:T(8,128)(2,1)}, bf16[128,2048]{1,0:T(8,128)(2,1)}, u32[]{:S(2)}, u32[]{:S(2)}) %collective-permute-start.1) | collective-permute-done | bytes 524320 | tf_op jit(solution)/shard_map/while/body/eval_jaxpr/ppermute | solution.py:16
  270.7 10.4 %collective-permute-done.1 = bf16[128,2048]{1,0:T(8,128)(2,1)} collective-permute-done((bf16[128,2048]{1,0:T(8,128)(2,1)}, bf16[128,2048]{1,0:T(8,128)(2,1)}, u32[]{:S(2)}, u32[]{:S(2)}) %collective-permute-start.1) | collective-permute-done | bytes 524320 | tf_op jit(solution)/shard_map/while/body/eval_jaxpr/ppermute | solution.py:16
  289.8 11.6 %collective-permute-done.1 = bf16[128,2048]{1,0:T(8,128)(2,1)} collective-permute-done((bf16[128,2048]{1,0:T(8,128)(2,1)}, bf16[128,2048]{1,0:T(8,128)(2,1)}, u32[]{:S(2)}, u32[]{:S(2)}) %collective-permute-start.1) | collective-permute-done | bytes 524320 | tf_op jit(solution)/shard_map/while/body/eval_jaxpr/ppermute | solution.py:16
  310.1 6.2 collective-permute-done.1
  321.8 42.5 %while.61 = (s32[]{:T(128)}, f32[128,32,64]{0,2,1:T(8,128)S(1)}, bf16[2,256,32,64]{1,3,2,0:T(8,128)(2,1)}, f32[2,128,32,64]{1,3,2,0:T(8,128)}, f32[2,256,32]{1,2...) while((s32[]{:T(128)}, f32[128,32,64]{0,2,1:T(8,128)S(1)}, ...), condition=%wide.region_9.10_spmd.clone, body=%wide.region_6.9_spmd.clone.sunk | while | flops 3331342336 | bytes 75240664 | solution.py:52
  331.9 9.8 %bitcast_dynamic-update-slice_fusion.7 = bf16[2,256,32,64]{1,3,2,0:T(8,128)(2,1)S(1)} fusion(bf16[2,256,32,64]{1,3,2,0:T(8,128)(2,1)S(1)} %copy-done.21, s32[]{:T(128)S(6)} %copy.238, f32[256,32,64]{0,2,1:T(8,128)S(1)} %bitcast.378, f32[256,256]{1,0:T(8,128)S(1)} %fusion.184, f32[32,256]{1,0:T(8,128)S(1)} %get-tuple-element.917, ...), kind=kOutput, calls=%fused_computation.75.clone.1 | convolution fusion | flops 1617952768 | bytes 6718464 | tf_op jit(solution)/shard_map/jvp()/while/body/eval_jaxpr/hij,jhp->ihp/dot_general | solution.py:29
  353.2 9.8 %bitcast_dynamic-update-slice_fusion.7 = bf16[2,256,32,64]{1,3,2,0:T(8,128)(2,1)S(1)} fusion(bf16[2,256,32,64]{1,3,2,0:T(8,128)(2,1)S(1)} %copy-done.21, s32[]{:T(128)S(6)} %copy.238, f32[256,32,64]{0,2,1:T(8,128)S(1)} %bitcast.378, f32[256,256]{1,0:T(8,128)S(1)} %fusion.184, f32[32,256]{1,0:T(8,128)S(1)} %get-tuple-element.917, ...), kind=kOutput, calls=%fused_computation.75.clone.1 | convolution fusion | flops 1617952768 | bytes 6718464 | tf_op jit(solution)/shard_map/jvp()/while/body/eval_jaxpr/hij,jhp->ihp/dot_general | solution.py:29
  367.8 162.2 %while.60 = (s32[]{:T(128)}, f32[128,32,64]{0,2,1:T(8,128)}, bf16[2,256,32,64]{1,3,2,0:T(8,128)(2,1)}, bf16[2,256,128]{2,1,0:T(8,128)(2,1)}, bf16[2,256,128]{2,1...) while((s32[]{:T(128)}, f32[128,32,64]{0,2,1:T(8,128)}, ...), condition=%wide.region_22.23_spmd, body=%wide.region_10.22_spmd.sunk | while | flops 7582384128 | bytes 121510040 | solution.py:52
  402.0 14.0 %fusion.171 = (f32[32,256]{1,0:T(8,128)}, f32[32,256]{1,0:T(8,128)}, f32[256,256]{1,0:T(8,128)}) fusion(f32[256,256]{1,0:T(8,128)S(1)} %fusion.169, f32[32,256]{1,0:T(8,128)} %copy_bitcast_fusion.14, pred[256,256]{1,0:T(8,128)(4,1)} %iota_compare_fusion.3, f32[256,32,64]{0,2,1:T(8,128)} %get-tuple-element.893, f32[256,32,64]{0,2,1:T(8,128)} %get-tuple-element.890), kind=kOutput, calls=%fused_computation.15.clone.1 | convolution fusion | flops 1629405184 | bytes 4882432 | tf_op jit(solution)/shard_map/transpose(jvp())/while/body/eval_jaxpr/checkpoint/hij,jhp->ihp/dot_general | solution.py:29
  439.6 9.5 %bitcast_dynamic-update-slice_fusion.6 = bf16[2,256,32,64]{1,3,2,0:T(8,128)(2,1)} fusion(bf16[2,256,32,64]{1,3,2,0:T(8,128)(2,1)} %get-tuple-element.1013, s32[]{:T(128)S(6)} %sub.189, f32[256,32,64]{0,2,1:T(8,128)} %bitcast.379, f32[256,256]{1,0:T(8,128)S(1)} %copy-done.24, f32[32,256]{1,0:T(8,128)} %copy_bitcast_fusion.14, ...), kind=kOutput, calls=%fused_computation.22.clone.1 | convolution fusion | flops 1617952768 | bytes 6717444 | tf_op jit(solution)/shard_map/transpose(jvp())/while/body/eval_jaxpr/checkpoint/hij,jhp->ihp/dot_general | solution.py:29
  473.8 14.0 %fusion.171 = (f32[32,256]{1,0:T(8,128)}, f32[32,256]{1,0:T(8,128)}, f32[256,256]{1,0:T(8,128)}) fusion(f32[256,256]{1,0:T(8,128)S(1)} %fusion.169, f32[32,256]{1,0:T(8,128)} %copy_bitcast_fusion.14, pred[256,256]{1,0:T(8,128)(4,1)} %iota_compare_fusion.3, f32[256,32,64]{0,2,1:T(8,128)} %get-tuple-element.893, f32[256,32,64]{0,2,1:T(8,128)} %get-tuple-element.890), kind=kOutput, calls=%fused_computation.15.clone.1 | convolution fusion | flops 1629405184 | bytes 4882432 | tf_op jit(solution)/shard_map/transpose(jvp())/while/body/eval_jaxpr/checkpoint/hij,jhp->ihp/dot_general | solution.py:29
  511.4 9.5 %bitcast_dynamic-update-slice_fusion.6 = bf16[2,256,32,64]{1,3,2,0:T(8,128)(2,1)} fusion(bf16[2,256,32,64]{1,3,2,0:T(8,128)(2,1)} %get-tuple-element.1013, s32[]{:T(128)S(6)} %sub.189, f32[256,32,64]{0,2,1:T(8,128)} %bitcast.379, f32[256,256]{1,0:T(8,128)S(1)} %copy-done.24, f32[32,256]{1,0:T(8,128)} %copy_bitcast_fusion.14, ...), kind=kOutput, calls=%fused_computation.22.clone.1 | convolution fusion | flops 1617952768 | bytes 6717444 | tf_op jit(solution)/shard_map/transpose(jvp())/while/body/eval_jaxpr/checkpoint/hij,jhp->ihp/dot_general | solution.py:29
  534.4 6.8 convert_bitcast_fusion
  542.6 7.4 %copy.147 = bf16[2,256,32,64]{3,2,1,0:T(8,128)(2,1)} copy(bf16[2,256,32,64]{1,3,2,0:T(8,128)(2,1)} %get-tuple-element.378) | data formatting | bytes 4194304
  550.1 6.8 reshape.329
  560.1 129.8 %reduce-scatter.2.cloned.1.call-done = bf16[256,2048]{0,1:T(8,128)(2,1)} async-done(((bf16[2048,2048]{0,1:T(8,128)(2,1)}), bf16[256,2048]{0,1:T(8,128)(2,1)}) %reduce-scatter.2.cloned.1.call-update) | async-done | bytes 1048592 | tf_op jit(solution)/shard_map/reduce_scatter | solution.py:105
  (366 shorter events, 268.9 us)
Async XLA Ops:
  8.0 18.5 %copy-start = (bf16[512,2048]{1,0:T(8,128)(2,1)S(1)}, bf16[512,2048]{1,0:T(8,128)(2,1)}, u32[]{:S(2)}) copy-start(bf16[512,2048]{1,0:T(8,128)(2,1)} %param.18) | copy-start | bytes 6291460
  8.0 548.8 %all-reduce.5.cloned.1.call-start = ((), (), s32[]{:S(2)}) async-start(), calls=%async_computation.2 | async-start | bytes 524288 | tf_op jit(solution)/shard_map/psum | solution.py:114
  54.0 17.1 %collective-permute-start = (bf16[128,2048]{1,0:T(8,128)(2,1)}, bf16[128,2048]{1,0:T(8,128)(2,1)}, u32[]{:S(2)}, u32[]{:S(2)}) collective-permute-start(bf16[128,2048]{1,0:T(8,128)(2,1)} %fusion.185), channel_id=1, source_target_pairs={{2,0},{4,2},{6,4},{8,6},{10,8},{12,10},{14,12},{3,1},{5,3},{7,5},{... | collective-permute-start | bytes 1572872 | tf_op jit(solution)/shard_map/while/body/eval_jaxpr/ppermute | solution.py:16
  75.8 15.9 %collective-permute-start = (bf16[128,2048]{1,0:T(8,128)(2,1)}, bf16[128,2048]{1,0:T(8,128)(2,1)}, u32[]{:S(2)}, u32[]{:S(2)}) collective-permute-start(bf16[128,2048]{1,0:T(8,128)(2,1)} %fusion.185), channel_id=1, source_target_pairs={{2,0},{4,2},{6,4},{8,6},{10,8},{12,10},{14,12},{3,1},{5,3},{7,5},{... | collective-permute-start | bytes 1572872 | tf_op jit(solution)/shard_map/while/body/eval_jaxpr/ppermute | solution.py:16
  96.5 15.0 %collective-permute-start = (bf16[128,2048]{1,0:T(8,128)(2,1)}, bf16[128,2048]{1,0:T(8,128)(2,1)}, u32[]{:S(2)}, u32[]{:S(2)}) collective-permute-start(bf16[128,2048]{1,0:T(8,128)(2,1)} %fusion.185), channel_id=1, source_target_pairs={{2,0},{4,2},{6,4},{8,6},{10,8},{12,10},{14,12},{3,1},{5,3},{7,5},{... | collective-permute-start | bytes 1572872 | tf_op jit(solution)/shard_map/while/body/eval_jaxpr/ppermute | solution.py:16
  116.2 14.0 %collective-permute-start = (bf16[128,2048]{1,0:T(8,128)(2,1)}, bf16[128,2048]{1,0:T(8,128)(2,1)}, u32[]{:S(2)}, u32[]{:S(2)}) collective-permute-start(bf16[128,2048]{1,0:T(8,128)(2,1)} %fusion.185), channel_id=1, source_target_pairs={{2,0},{4,2},{6,4},{8,6},{10,8},{12,10},{14,12},{3,1},{5,3},{7,5},{... | collective-permute-start | bytes 1572872 | tf_op jit(solution)/shard_map/while/body/eval_jaxpr/ppermute | solution.py:16
  135.0 13.1 %collective-permute-start = (bf16[128,2048]{1,0:T(8,128)(2,1)}, bf16[128,2048]{1,0:T(8,128)(2,1)}, u32[]{:S(2)}, u32[]{:S(2)}) collective-permute-start(bf16[128,2048]{1,0:T(8,128)(2,1)} %fusion.185), channel_id=1, source_target_pairs={{2,0},{4,2},{6,4},{8,6},{10,8},{12,10},{14,12},{3,1},{5,3},{7,5},{... | collective-permute-start | bytes 1572872 | tf_op jit(solution)/shard_map/while/body/eval_jaxpr/ppermute | solution.py:16
  152.8 12.2 %collective-permute-start = (bf16[128,2048]{1,0:T(8,128)(2,1)}, bf16[128,2048]{1,0:T(8,128)(2,1)}, u32[]{:S(2)}, u32[]{:S(2)}) collective-permute-start(bf16[128,2048]{1,0:T(8,128)(2,1)} %fusion.185), channel_id=1, source_target_pairs={{2,0},{4,2},{6,4},{8,6},{10,8},{12,10},{14,12},{3,1},{5,3},{7,5},{... | collective-permute-start | bytes 1572872 | tf_op jit(solution)/shard_map/while/body/eval_jaxpr/ppermute | solution.py:16
  169.8 12.1 %collective-permute-start = (bf16[128,2048]{1,0:T(8,128)(2,1)}, bf16[128,2048]{1,0:T(8,128)(2,1)}, u32[]{:S(2)}, u32[]{:S(2)}) collective-permute-start(bf16[128,2048]{1,0:T(8,128)(2,1)} %fusion.185), channel_id=1, source_target_pairs={{2,0},{4,2},{6,4},{8,6},{10,8},{12,10},{14,12},{3,1},{5,3},{7,5},{... | collective-permute-start | bytes 1572872 | tf_op jit(solution)/shard_map/while/body/eval_jaxpr/ppermute | solution.py:16
  186.5 4.9 copy-start.34
  199.4 11.8 %collective-permute-start.1 = (bf16[128,2048]{1,0:T(8,128)(2,1)}, bf16[128,2048]{1,0:T(8,128)(2,1)}, u32[]{:S(2)}, u32[]{:S(2)}) collective-permute-start(bf16[128,2048]{1,0:T(8,128)(2,1)} %fusion.186), channel_id=1, source_target_pairs={{0,2},{2,4},{4,6},{6,8},{8,10},{10,12},{12,14},{1,3},{3,5},{5,7},{... | collective-permute-start | bytes 1572872 | tf_op jit(solution)/shard_map/while/body/eval_jaxpr/ppermute | solution.py:16
  214.7 12.4 %collective-permute-start.1 = (bf16[128,2048]{1,0:T(8,128)(2,1)}, bf16[128,2048]{1,0:T(8,128)(2,1)}, u32[]{:S(2)}, u32[]{:S(2)}) collective-permute-start(bf16[128,2048]{1,0:T(8,128)(2,1)} %fusion.186), channel_id=1, source_target_pairs={{0,2},{2,4},{4,6},{6,8},{8,10},{10,12},{12,14},{1,3},{3,5},{5,7},{... | collective-permute-start | bytes 1572872 | tf_op jit(solution)/shard_map/while/body/eval_jaxpr/ppermute | solution.py:16
  230.6 13.5 %collective-permute-start.1 = (bf16[128,2048]{1,0:T(8,128)(2,1)}, bf16[128,2048]{1,0:T(8,128)(2,1)}, u32[]{:S(2)}, u32[]{:S(2)}) collective-permute-start(bf16[128,2048]{1,0:T(8,128)(2,1)} %fusion.186), channel_id=1, source_target_pairs={{0,2},{2,4},{4,6},{6,8},{8,10},{10,12},{12,14},{1,3},{3,5},{5,7},{... | collective-permute-start | bytes 1572872 | tf_op jit(solution)/shard_map/while/body/eval_jaxpr/ppermute | solution.py:16
  247.5 14.5 %collective-permute-start.1 = (bf16[128,2048]{1,0:T(8,128)(2,1)}, bf16[128,2048]{1,0:T(8,128)(2,1)}, u32[]{:S(2)}, u32[]{:S(2)}) collective-permute-start(bf16[128,2048]{1,0:T(8,128)(2,1)} %fusion.186), channel_id=1, source_target_pairs={{0,2},{2,4},{4,6},{6,8},{8,10},{10,12},{12,14},{1,3},{3,5},{5,7},{... | collective-permute-start | bytes 1572872 | tf_op jit(solution)/shard_map/while/body/eval_jaxpr/ppermute | solution.py:16
  265.5 15.6 %collective-permute-start.1 = (bf16[128,2048]{1,0:T(8,128)(2,1)}, bf16[128,2048]{1,0:T(8,128)(2,1)}, u32[]{:S(2)}, u32[]{:S(2)}) collective-permute-start(bf16[128,2048]{1,0:T(8,128)(2,1)} %fusion.186), channel_id=1, source_target_pairs={{0,2},{2,4},{4,6},{6,8},{8,10},{10,12},{12,14},{1,3},{3,5},{5,7},{... | collective-permute-start | bytes 1572872 | tf_op jit(solution)/shard_map/while/body/eval_jaxpr/ppermute | solution.py:16
  284.6 16.8 %collective-permute-start.1 = (bf16[128,2048]{1,0:T(8,128)(2,1)}, bf16[128,2048]{1,0:T(8,128)(2,1)}, u32[]{:S(2)}, u32[]{:S(2)}) collective-permute-start(bf16[128,2048]{1,0:T(8,128)(2,1)} %fusion.186), channel_id=1, source_target_pairs={{0,2},{2,4},{4,6},{6,8},{8,10},{10,12},{12,14},{1,3},{3,5},{5,7},{... | collective-permute-start | bytes 1572872 | tf_op jit(solution)/shard_map/while/body/eval_jaxpr/ppermute | solution.py:16
  304.9 11.4 %collective-permute-start.1 = (bf16[128,2048]{1,0:T(8,128)(2,1)}, bf16[128,2048]{1,0:T(8,128)(2,1)}, u32[]{:S(2)}, u32[]{:S(2)}) collective-permute-start(bf16[128,2048]{1,0:T(8,128)(2,1)} %fusion.186), channel_id=1, source_target_pairs={{0,2},{2,4},{4,6},{6,8},{8,10},{10,12},{12,14},{1,3},{3,5},{5,7},{... | collective-permute-start | bytes 1572872 | tf_op jit(solution)/shard_map/while/body/eval_jaxpr/ppermute | solution.py:16
  402.0 14.1 %copy-start.23 = (f32[256,256]{1,0:T(8,128)}, f32[256,256]{1,0:T(8,128)S(1)}, u32[]{:S(2)}) copy-start(f32[256,256]{1,0:T(8,128)S(1)} %fusion.169) | copy-start | bytes 786436 | tf_op jit(solution)/shard_map/transpose(jvp())/while
  425.9 5.2 copy-start.10
  425.9 5.2 copy-start.30
  425.9 6.3 copy-start.1
  439.6 9.6 %copy-start.3 = (f32[256,32,64]{0,2,1:T(8,128)S(1)}, f32[256,32,64]{0,2,1:T(8,128)}, u32[]{:S(2)}) copy-start(f32[256,32,64]{0,2,1:T(8,128)} %get-tuple-element.893) | copy-start | bytes 6291460 | tf_op jit(solution)/shard_map/transpose(jvp())/while
  439.6 9.5 %copy-start.5 = (f32[128,32,64]{0,2,1:T(8,128)S(1)}, f32[128,32,64]{0,2,1:T(8,128)}, u32[]{:S(2)}) copy-start(f32[128,32,64]{0,2,1:T(8,128)} %get-tuple-element.887) | copy-start | bytes 3145732 | tf_op jit(solution)/shard_map/transpose(jvp())/while
  452.7 5.3 copy-start.26
  473.7 14.1 %copy-start.23 = (f32[256,256]{1,0:T(8,128)}, f32[256,256]{1,0:T(8,128)S(1)}, u32[]{:S(2)}) copy-start(f32[256,256]{1,0:T(8,128)S(1)} %fusion.169) | copy-start | bytes 786436 | tf_op jit(solution)/shard_map/transpose(jvp())/while
  497.7 5.2 copy-start.10
  497.7 5.2 copy-start.30
  497.7 6.3 copy-start.1
  511.4 9.6 %copy-start.3 = (f32[256,32,64]{0,2,1:T(8,128)S(1)}, f32[256,32,64]{0,2,1:T(8,128)}, u32[]{:S(2)}) copy-start(f32[256,32,64]{0,2,1:T(8,128)} %get-tuple-element.893) | copy-start | bytes 6291460 | tf_op jit(solution)/shard_map/transpose(jvp())/while
  511.4 9.5 %copy-start.5 = (f32[128,32,64]{0,2,1:T(8,128)S(1)}, f32[128,32,64]{0,2,1:T(8,128)}, u32[]{:S(2)}) copy-start(f32[128,32,64]{0,2,1:T(8,128)} %get-tuple-element.887) | copy-start | bytes 3145732 | tf_op jit(solution)/shard_map/transpose(jvp())/while
  524.5 5.3 copy-start.26
  530.0 159.9 %reduce-scatter.2.cloned.1.call-start = ((), (), s32[]{:S(2)}) async-start(), calls=%async_computation.1 | async-start | bytes 9437184 | tf_op jit(solution)/shard_map/reduce_scatter | solution.py:105
  (55 other events, 153.4 us)
Sparse Core Ops, SparseCore 0:
  530.1 19.5 all-reduce.4
Sparse Core Ops, SparseCore 1:
  541.3 148.6 reduce-scatter.1
where the time goes:
time: 712 us; the launch traced here: 700 us
  waiting for transfers between devices  279 us (39%)
  matrix products  144 us (20%)
  local copies, waits for them, and re-layouts  111 us (16%)
  other arithmetic  83.6 us (12%)
  starting transfers between devices  46.1 us (6%)
  loops' own time  20.1 us (3%)
  between operations  16 us (2%)
    ppermute x14, waiting for transfers between devices, from_behind(): return lax.ppermute(x, axis, pairs)  149 us
    reduce_scatter x1, waiting for transfers between devices, on_device(): lax.psum_scatter(lax.dot_general(dout, y_half, (((0,), (0,)), ((), ())),...  130 us
    dot_general x6, matrix products, block_forward(): inside = jnp.einsum('hij,jhp->ihp', weights, x_block, precision=highest)  66.7 us
    ppermute x14, starting transfers between devices, from_behind(): return lax.ppermute(x, axis, pairs)  46 us
    unnamed x27, local copies, waits for them, and re-layouts  33.6 us
    while x10, matrix products  28.5 us
    another operation x2, loops' own time, local_forward(): lax.scan(advance, start_state, (x_blocks, b_blocks, c_blocks, l_blocks))  19.6 us
    convert_element_type x7, other arithmetic, backward_turn(): outgoing.astype(jnp.bfloat16)  17.1 us
  transfers between devices with their start and end apart: 16, of which 15 were waited for; matrix products, arithmetic and copies ran while one was open for 4% of the time, Pallas kernels for 0%

commit v1 on v0

v1 whole, which is shorter than its diff:
```python
import functools
import math

import jax
import jax.numpy as jnp
from jax import lax
from jax.experimental import pallas as pl
from jax.experimental.pallas import tpu as pltpu
from jax.sharding import PartitionSpec as P

BLOCK = 128
LANES = 128
GROUP_HEADS = 8
LOG2E = math.log2(math.e)
F32 = jnp.float32
BF16 = jnp.bfloat16
EXACT = lax.Precision.HIGHEST
NT = (((1,), (1,)), ((), ()))
TN = (((0,), (0,)), ((), ()))
MIB = 2**20


def dot(a, b, dims=(((1,), (0,)), ((), ())), precision=None):
    return lax.dot_general(a, b, dims, precision=precision, preferred_element_type=F32)


def low_lanes(rows):
    return lax.broadcasted_iota(jnp.int32, (rows, LANES), 1) < LANES // 2


def pair_columns(small, pair):
    rows = small.shape[0]
    even = jnp.broadcast_to(small[:, 2 * pair : 2 * pair + 1], (rows, LANES))
    odd = jnp.broadcast_to(small[:, 2 * pair + 1 : 2 * pair + 2], (rows, LANES))
    return jnp.where(low_lanes(rows), even, odd)


def transposed(x):
    return x.astype(F32).T.astype(BF16)


def start_kernel(q_ref, loga_ref, x_ref, b_ref, cum_ref, cumt_ref, lead_ref, send_ref, keep_ref, tot_ref, own):
    rows, heads = loga_ref.shape
    width = x_ref.shape[1]
    half = width // 2
    states = b_ref.shape[1]
    r = lax.broadcasted_iota(jnp.int32, (BLOCK, BLOCK), 0)
    c = lax.broadcasted_iota(jnp.int32, (BLOCK, BLOCK), 1)
    tri = (r >= c).astype(F32)
    eye = (
        lax.broadcasted_iota(jnp.int32, (heads, heads), 0)
        == lax.broadcasted_iota(jnp.int32, (heads, heads), 1)
    ).astype(F32)
    base = jnp.zeros((1, heads), F32)
    whole = []
    for k in range(rows // BLOCK):
        at = slice(k * BLOCK, (k + 1) * BLOCK)
        cum = dot(tri, loga_ref[at, :] * LOG2E, precision=EXACT)
        for g in range(heads // GROUP_HEADS):
            hs = slice(g * GROUP_HEADS, (g + 1) * GROUP_HEADS)
            cum_ref[g, at, :] = cum[:, hs]
        cumt_ref[:, at] = dot(eye, cum, NT, precision=EXACT)
        whole.append(cum + base)
        base = base + cum[BLOCK - 1 :, :]
    for k, cum in enumerate(whole):
        at = slice(k * BLOCK, (k + 1) * BLOCK)
        lead = jnp.exp2(cum)
        for g in range(heads // GROUP_HEADS):
            hs = slice(g * GROUP_HEADS, (g + 1) * GROUP_HEADS)
            lead_ref[g, at, :] = lead[:, hs]
    tails = [jnp.exp2(base - cum) for cum in whole]
    b_t = transposed(b_ref[...])
    total = jnp.broadcast_to(base, (8, heads))
    for p in range(heads // 2):
        ps = slice(p * LANES, (p + 1) * LANES)
        xs = jnp.concatenate(
            [
                (x_ref[k * BLOCK : (k + 1) * BLOCK, ps].astype(F32) * pair_columns(t, p)).astype(BF16)
                for k, t in enumerate(tails)
            ],
            axis=0,
        )
        own[0:states, ps] = dot(b_t, xs)
        own[states : states + 8, ps] = pair_columns(total, p)
    q = q_ref[0]
    mine = pl.ds(pl.multiple_of(q * half, LANES), half)
    other = pl.ds(pl.multiple_of((1 - q) * half, LANES), half)
    keep_ref[...] = own[0:states, mine]
    tot_ref[...] = own[states : states + 8, mine]
    send_ref[0:states, :] = own[0:states, other].astype(BF16)
    t = own[states : states + 8, other]
    hi = t.astype(BF16)
    mid = (t - hi.astype(F32)).astype(BF16)
    lo = (t - hi.astype(F32) - mid.astype(F32)).astype(BF16)
    row = lax.broadcasted_iota(jnp.int32, (8, half), 0)
    pieces = jnp.where(
        row == 0, hi.astype(F32), jnp.where(row == 1, mid.astype(F32), jnp.where(row == 2, lo.astype(F32), 0.0))
    )
    send_ref[states : states + 16, :] = jnp.concatenate([pieces, jnp.zeros_like(pieces)], axis=0).astype(BF16)


def start(q, loga, x, b):
    rows, heads = loga.shape
    width = x.shape[1]
    states = b.shape[1]
    groups = heads // GROUP_HEADS
    vmem = pl.BlockSpec(memory_space=pltpu.VMEM)
    return pl.pallas_call(
        start_kernel,
        in_specs=[pl.BlockSpec(memory_space=pltpu.SMEM), vmem, vmem, vmem],
        out_specs=[vmem] * 6,
        out_shape=[
            jax.ShapeDtypeStruct((groups, rows, GROUP_HEADS), F32),
            jax.ShapeDtypeStruct((heads, rows), F32),
            jax.ShapeDtypeStruct((groups, rows, GROUP_HEADS), F32),
            jax.ShapeDtypeStruct((states + 16, width // 2), BF16),
            jax.ShapeDtypeStruct((states, width // 2), F32),
            jax.ShapeDtypeStruct((8, width // 2), F32),
        ],
        scratch_shapes=[pltpu.VMEM((states + 8, width), F32)],
        compiler_params=pltpu.CompilerParams(vmem_limit_bytes=24 * MIB),
        cost_estimate=pl.CostEstimate(flops=10**9, bytes_accessed=6 * MIB, transcendentals=10**5),
        name="start",
    )(q, loga, x, b)


def block_diagonal(pair):
    low = low_lanes(pair.shape[0])
    wide = pair.astype(F32)
    zero = jnp.zeros_like(wide)
    return jnp.concatenate([jnp.where(low, wide, zero), jnp.where(low, zero, wide)], axis=0).astype(BF16)


def forward_kernel(x_ref, b_ref, c_ref, cum_ref, cumt_ref, y_ref, scores):
    rows = x_ref.shape[0]
    blocks = rows // BLOCK

    @pl.when(pl.program_id(0) == 0)
    def _():
        r = lax.broadcasted_iota(jnp.int32, (BLOCK, BLOCK), 0)
        c = lax.broadcasted_iota(jnp.int32, (BLOCK, BLOCK), 1)
        for k in range(blocks):
            at = slice(k * BLOCK, (k + 1) * BLOCK)
            scores[k] = jnp.where(r >= c, dot(c_ref[at, :], b_ref[at, :], NT), 0.0)

    low = low_lanes(BLOCK)
    b_t = [transposed(b_ref[k * BLOCK : (k + 1) * BLOCK, :]) for k in range(blocks)]
    for p in range(GROUP_HEADS // 2):
        ps = slice(p * LANES, (p + 1) * LANES)
        state = None
        for k in range(blocks):
            at = slice(k * BLOCK, (k + 1) * BLOCK)
            a0 = jnp.broadcast_to(cum_ref[0, at, 2 * p : 2 * p + 1], (BLOCK, LANES))
            a1 = jnp.broadcast_to(cum_ref[0, at, 2 * p + 1 : 2 * p + 2], (BLOCK, LANES))
            r0 = cumt_ref[2 * p : 2 * p + 1, at]
            r1 = cumt_ref[2 * p + 1 : 2 * p + 2, at]
            s = scores[k]
            w0 = jnp.exp2(jnp.minimum(a0 - r0, 0.0)) * s
            w1 = jnp.exp2(jnp.minimum(a1 - r1, 0.0)) * s
            x = x_ref[at, ps]
            y = dot(jnp.concatenate([w0, w1], axis=1).astype(BF16), block_diagonal(x))
            both = jnp.where(low, a0, a1)
            if k > 0:
                y = y + jnp.exp2(both) * dot(c_ref[at, :], state.astype(BF16))
            if k < blocks - 1:
                last = both[BLOCK - 1 :, :]
                fresh = dot(b_t[k], (x.astype(F32) * jnp.exp2(last - both)).astype(BF16))
                state = fresh if k == 0 else jnp.exp2(last) * state + fresh
            y_ref[at, ps] = y


def forward(x, b, c, cum, cumt):
    rows, width = x.shape
    groups = cum.shape[0]
    wide = width // groups
    return pl.pallas_call(
        forward_kernel,
        grid=(groups,),
        in_specs=[
            pl.BlockSpec((rows, wide), lambda g: (0, g)),
            pl.BlockSpec(b.shape, lambda g: (0, 0)),
            pl.BlockSpec(c.shape, lambda g: (0, 0)),
            pl.BlockSpec((1, rows, GROUP_HEADS), lambda g: (g, 0, 0)),
            pl.BlockSpec((GROUP_HEADS, rows), lambda g: (g, 0)),
        ],
        out_specs=pl.BlockSpec((rows, wide), lambda g: (0, g)),
        out_shape=jax.ShapeDtypeStruct((rows, width), F32),
        scratch_shapes=[pltpu.VMEM((rows // BLOCK, BLOCK, BLOCK), F32)],
        compiler_params=pltpu.CompilerParams(vmem_limit_bytes=24 * MIB),
        cost_estimate=pl.CostEstimate(flops=6 * 10**9, bytes_accessed=7 * MIB, transcendentals=3 * 10**6),
        name="forward",
    )(x, b, c, cum, cumt)


def finish_kernel(y_ref, c_ref, lead_ref, state_ref, out_ref):
    for p in range(GROUP_HEADS // 2):
        ps = slice(p * LANES, (p + 1) * LANES)
        lead = pair_columns(lead_ref[0], p)
        out_ref[:, ps] = (y_ref[:, ps] + lead * dot(c_ref[...], state_ref[:, ps])).astype(BF16)


def finish(y, c, lead, state):
    rows, width = y.shape
    groups = lead.shape[0]
    wide = width // groups
    return pl.pallas_call(
        finish_kernel,
        grid=(groups,),
        in_specs=[
            pl.BlockSpec((rows, wide), lambda g: (0, g)),
            pl.BlockSpec(c.shape, lambda g: (0, 0)),
            pl.BlockSpec((1, rows, GROUP_HEADS), lambda g: (g, 0, 0)),
            pl.BlockSpec((state.shape[0], wide), lambda g: (0, g)),
        ],
        out_specs=pl.BlockSpec((rows, wide), lambda g: (0, g)),
        out_shape=jax.ShapeDtypeStruct((rows, width), BF16),
        compiler_params=pltpu.CompilerParams(vmem_limit_bytes=16 * MIB),
        cost_estimate=pl.CostEstimate(flops=3 * 10**8, bytes_accessed=7 * MIB, transcendentals=0),
        name="finish",
    )(y, c, lead, state)


def adjoint_kernel(dout_ref, w_ref, c_ref, lead_ref, gy_ref, own_ref):
    c_t = transposed(c_ref[...])
    gy = dot(dout_ref[...], w_ref[...])
    gy_ref[...] = gy.astype(BF16)
    for p in range(GROUP_HEADS // 2):
        ps = slice(p * LANES, (p + 1) * LANES)
        scaled = gy[:, ps] * pair_columns(lead_ref[0], p)
        own_ref[:, ps] = dot(c_t, scaled.astype(BF16))


def adjoint(dout, w, c, lead):
    rows, model = dout.shape
    width = w.shape[1]
    groups = lead.shape[0]
    wide = width // groups
    states = c.shape[1]
    return pl.pallas_call(
        adjoint_kernel,
        grid=(groups,),
        in_specs=[
            pl.BlockSpec((rows, model), lambda g: (0, 0)),
            pl.BlockSpec((model, wide), lambda g: (0, g)),
            pl.BlockSpec(c.shape, lambda g: (0, 0)),
            pl.BlockSpec((1, rows, GROUP_HEADS), lambda g: (g, 0, 0)),
        ],
        out_specs=[
            pl.BlockSpec((rows, wide), lambda g: (0, g)),
            pl.BlockSpec((states, wide), lambda g: (0, g)),
        ],
        out_shape=[
            jax.ShapeDtypeStruct((rows, width), BF16),
            jax.ShapeDtypeStruct((states, width), F32),
        ],
        compiler_params=pltpu.CompilerParams(vmem_limit_bytes=24 * MIB),
        cost_estimate=pl.CostEstimate(flops=6 * 10**9, bytes_accessed=14 * MIB, transcendentals=0),
        name="adjoint",
    )(dout, w, c, lead)


def turn_kernel(order_ref, dout_ref, out_ref):
    out_ref[...] = transposed(dout_ref[...])


def turn(order, dout):
    rows, model = dout.shape
    count = order.shape[0]
    tall = model // count
    return pl.pallas_call(
        turn_kernel,
        grid_spec=pltpu.PrefetchScalarGridSpec(
            num_scalar_prefetch=1,
            grid=(count,),
            in_specs=[pl.BlockSpec((rows, tall), lambda i, order: (0, order[i]))],
            out_specs=pl.BlockSpec((tall, rows), lambda i, order: (i, 0)),
        ),
        out_shape=jax.ShapeDtypeStruct((model, rows), BF16),
        compiler_params=pltpu.CompilerParams(vmem_limit_bytes=16 * MIB),
        cost_estimate=pl.CostEstimate(flops=0, bytes_accessed=4 * MIB, transcendentals=0),
        name="turn",
    )(order, dout)


def backward_kernel(
    x_ref, gy_ref, y_ref, b_ref, c_ref, cum_ref, cumt_ref, s_ref, g_ref,
    gx_ref, db_ref, dc_ref, dl_ref,
    scores, dscores,
):
    rows = x_ref.shape[0]
    blocks = rows // BLOCK
    step, steps = pl.program_id(0), pl.num_programs(0)
    r = lax.broadcasted_iota(jnp.int32, (BLOCK, BLOCK), 0)
    c = lax.broadcasted_iota(jnp.int32, (BLOCK, BLOCK), 1)
    upper = r <= c

    @pl.when(step == 0)
    def _():
        for k in range(blocks):
            at = slice(k * BLOCK, (k + 1) * BLOCK)
            scores[k] = jnp.where(upper, dot(b_ref[at, :], c_ref[at, :], NT), 0.0)
        dscores[...] = jnp.zeros_like(dscores)
        db_ref[...] = jnp.zeros_like(db_ref)
        dc_ref[...] = jnp.zeros_like(dc_ref)

    low = low_lanes(BLOCK)
    spots = [slice(k * BLOCK, (k + 1) * BLOCK) for k in range(blocks)]
    b_t = [transposed(b_ref[at, :]) for at in spots]
    c_t = [transposed(c_ref[at, :]) for at in spots]
    sums = [jnp.zeros((GROUP_HEADS, BLOCK), F32)] * blocks
    head_row = lax.broadcasted_iota(jnp.int32, (GROUP_HEADS, LANES), 0)
    head_half = lax.broadcasted_iota(jnp.int32, (GROUP_HEADS, LANES), 1) // (LANES // 2)
    for p in range(GROUP_HEADS // 2):
        ps = slice(p * LANES, (p + 1) * LANES)
        place = (head_row == 2 * p + head_half).astype(BF16)
        columns, tails, entering = [], [], [s_ref[:, ps].astype(F32)]
        for k, at in enumerate(spots):
            a0 = jnp.broadcast_to(cum_ref[0, at, 2 * p : 2 * p + 1], (BLOCK, LANES))
            a1 = jnp.broadcast_to(cum_ref[0, at, 2 * p + 1 : 2 * p + 2], (BLOCK, LANES))
            both = jnp.where(low, a0, a1)
            last = both[BLOCK - 1 :, :]
            columns.append((a0, a1, both, jnp.exp2(last)))
            tail = jnp.exp2(last - both)
            tails.append((tail, (x_ref[at, ps].astype(F32) * tail).astype(BF16)))
            entering.append(jnp.exp2(last) * entering[k] + dot(b_t[k], tails[k][1]))
        g = g_ref[:, ps].astype(F32)
        for k in reversed(range(blocks)):
            at = spots[k]
            a0, a1, both, span = columns[k]
            tail, xs = tails[k]
            d0 = jnp.exp2(jnp.minimum(cumt_ref[2 * p : 2 * p + 1, at] - a0, 0.0))
            d1 = jnp.exp2(jnp.minimum(cumt_ref[2 * p + 1 : 2 * p + 2, at] - a1, 0.0))
            s = scores[k]
            x, gy = x_ref[at, ps], gy_ref[at, ps]
            g_half = g.astype(BF16)
            weights = jnp.concatenate([d0 * s, d1 * s], axis=1).astype(BF16)
            gx = dot(weights, block_diagonal(gy)) + tail * dot(b_ref[at, :], g_half)
            gx_ref[at, ps] = gx.astype(BF16)
            dw = dot(block_diagonal(x), gy, NT)
            dscores[k] += d0 * dw[:BLOCK] + d1 * dw[BLOCK:]
            db_ref[at, :] += dot(xs, g_half, NT)
            gys = (gy.astype(F32) * jnp.exp2(both)).astype(BF16)
            dc_ref[at, :] += dot(gys, entering[k].astype(BF16), NT)
            term = gy.astype(F32) * y_ref[at, ps].astype(F32) - x.astype(F32) * gx
            end = jnp.sum(entering[k + 1] * g, axis=0, keepdims=True)
            term = term + jnp.where(r == BLOCK - 1, end, 0.0)
            hi = term.astype(BF16)
            lo = (term - hi.astype(F32)).astype(BF16)
            sums[k] = sums[k] + dot(place, hi, NT) + dot(place, lo, NT)
            g = span * g + dot(c_t[k], gys)
    for k, at in enumerate(spots):
        dl_ref[:, at] = dot(sums[k], (r >= c).astype(F32), precision=EXACT)

    @pl.when(step == steps - 1)
    def _():
        for k, at in enumerate(spots):
            ds = jnp.where(upper, dscores[k], 0.0)
            db_ref[at, :] += dot(ds.astype(BF16), c_ref[at, :])
            dc_ref[at, :] += dot(ds.T.astype(BF16), b_ref[at, :])


def backward(x, gy, y, b, c, cum, cumt, entering, leaving):
    rows, width = x.shape
    groups = cum.shape[0]
    heads = groups * GROUP_HEADS
    wide = width // groups
    states = b.shape[1]
    tall = pl.BlockSpec((rows, wide), lambda g: (0, g))
    whole = pl.BlockSpec((rows, states), lambda g: (0, 0))
    state = pl.BlockSpec((states, wide), lambda g: (0, g))
    return pl.pallas_call(
        backward_kernel,
        grid=(groups,),
        in_specs=[
            tall, tall, tall, whole, whole,
            pl.BlockSpec((1, rows, GROUP_HEADS), lambda g: (g, 0, 0)),
            pl.BlockSpec((GROUP_HEADS, rows), lambda g: (g, 0)),
            state, state,
        ],
        out_specs=[tall, whole, whole, pl.BlockSpec((GROUP_HEADS, rows), lambda g: (g, 0))],
        out_shape=[
            jax.ShapeDtypeStruct((rows, width), BF16),
            jax.ShapeDtypeStruct((rows, states), F32),
            jax.ShapeDtypeStruct((rows, states), F32),
            jax.ShapeDtypeStruct((heads, rows), F32),
        ],
        scratch_shapes=[pltpu.VMEM((rows // BLOCK, BLOCK, BLOCK), F32)] * 2,
        compiler_params=pltpu.CompilerParams(vmem_limit_bytes=24 * MIB),
        cost_estimate=pl.CostEstimate(flops=10**10, bytes_accessed=10 * MIB, transcendentals=3 * 10**6),
        name="backward",
    )(x, gy, y, b, c, cum, cumt, entering, leaving)


def ring_order(count):
    if count == 8:
        return [0, 2, 4, 6, 7, 5, 3, 1]
    return list(range(count))


def scan_states(keep, recv, my_total, other_total, first, up):
    count = lax.axis_size("ctx")
    by = 2 if up else -2
    pairs = [(i, i + by) for i in range(count) if 0 <= i + by < count]
    mine, others = jnp.exp2(my_total), jnp.exp2(other_total)
    recv = recv.astype(F32)
    both = jnp.where(first, others * keep + recv, mine * recv + keep)
    span = jnp.exp2(my_total + other_total)
    out = both
    for hop in range(count // 2 - 1):
        enter = lax.ppermute(out.astype(BF16), "ctx", pairs).astype(F32)
        if hop < count // 2 - 2:
            out = span * enter + both
    after_me, after_other = mine * enter + keep, others * enter + recv
    own = jnp.where(first, enter, after_other)
    partners = jnp.where(first, after_me, enter)
    return own.astype(BF16), partners.astype(BF16)


def on_device(x, b, c, loga, dout, w):
    count = lax.axis_size("ctx")
    me = lax.axis_index("ctx")
    q = lax.rem(me, 2)
    width = x.shape[1]
    half = width // 2
    states = b.shape[1]
    swap = [(i, i ^ 1) for i in range(count)]
    cum, cumt, lead, send, keep, total = start(q.reshape(1), loga, x, b)
    my_total = total[0:1]
    got = lax.ppermute(send, "ctx", swap)
    pieces = got[states : states + 3].astype(F32)
    other_total = pieces[0:1] + pieces[1:2] + pieces[2:3]
    own, partners = scan_states(keep, got[:states], my_total, other_total, q == 0, True)
    back = lax.ppermute(partners, "ctx", swap)
    entering = jnp.concatenate([jnp.where(q == 0, own, back), jnp.where(q == 0, back, own)], axis=1)

    y_local = forward(x, b, c, cum, cumt)
    gy, adj = adjoint(dout, w, c, lead)
    adj_keep = jnp.where(q == 0, adj[:, :half], adj[:, half:])
    adj_send = jnp.where(q == 0, adj[:, half:], adj[:, :half]).astype(BF16)
    adj_got = lax.ppermute(adj_send, "ctx", swap)
    own_g, partners_g = scan_states(adj_keep, adj_got, my_total, other_total, q == 1, False)
    back_g = lax.ppermute(partners_g, "ctx", swap)
    leaving = jnp.concatenate([jnp.where(q == 0, own_g, back_g), jnp.where(q == 0, back_g, own_g)], axis=1)

    ring = ring_order(count)
    places = [ring.index(i) for i in range(count)]
    at = jnp.asarray(places, jnp.int32)[me]
    order = jnp.asarray(ring, jnp.int32)[lax.rem(at + jnp.arange(count, dtype=jnp.int32), count)]
    dout_t = turn(order, dout)
    tall = dout.shape[1] // count

    y_half = finish(y_local, c, lead, entering)
    flows = []
    for f, by in enumerate((1, -1)):
        hops = [(ring[i], ring[(i + by) % count]) for i in range(count)]
        flows.append([hops, by, slice(f * half, (f + 1) * half), None])
    for step in range(count):
        for flow in flows:
            hops, by, cols, got_sum = flow
            offset = (by * (count - 1 - step)) % count
            part = dot(dout_t[offset * tall : (offset + 1) * tall], y_half[:, cols])
            if got_sum is not None:
                part = part + got_sum.astype(F32)
            flow[3] = part if step == count - 1 else lax.ppermute(part.astype(BF16), "ctx", hops)
    weight_grad = jnp.concatenate([flow[3] for flow in flows], axis=1)

    grad_x, db, dc, dl = backward(x, gy, y_half, b, c, cum, cumt, entering, leaving)
    terms = jnp.concatenate([db, dc], axis=0).astype(BF16)
    summed = terms.astype(F32) + lax.ppermute(terms, "head", [(0, 1), (1, 0)]).astype(F32)
    rows = x.shape[0]
    return grad_x, summed[:rows], summed[rows:], dl.T, weight_grad


def solution(mesh):
    tokens = ("group", "ctx")
    placed = (
        P(tokens, "head"),
        P(tokens, None),
        P(tokens, None),
        P(tokens, "head"),
        P(tokens, None),
        P(None, "head"),
    )
    return jax.shard_map(
        on_device,
        mesh=mesh,
        in_specs=placed,
        out_specs=(
            P(tokens, "head"),
            P(tokens, None),
            P(tokens, None),
            P(tokens, "head"),
            P(tokens, "head"),
        ),
        check_vma=False,
    )
```

time: 712 us -> 209 us (0.29); the launches traced: 700 us -> 208 us
  waiting for transfers between devices: 279 us -> 92 us
  matrix products: 144 us -> 7.03 us
  local copies, waits for them, and re-layouts: 111 us -> 14.1 us
  other arithmetic: 83.6 us -> 11 us
  Pallas kernels: 0 us -> 42.9 us
  loops' own time: 20.1 us -> 0 us
  between operations: 16 us -> 1.23 us
    reduce_scatter x1 -> x0, waiting for transfers between devices: 130 us -> none  [on_device(): lax.psum_scatter(lax.dot_general(dout, y_half, (((0,), (0,)), ((), ())),...]
    dot_general x22 -> x16, matrix products: 116 us -> 7.03 us  [dot(): lax.dot_general(a, b, dims, precision=precision, preferred_element_type=F32)]
    ppermute x14 -> x25, waiting for transfers between devices: 149 us -> 92 us  [the longest x14 67.2 us: on_device(): lax.ppermute(part.astype(BF16), 'ctx', hops)]
    convert_element_type x31 -> x8, other arithmetic: 62.5 us -> 6.9 us  [the longest x4 3.28 us: scan_states(): enter = lax.ppermute(out.astype(BF16), 'ctx', pairs).astype(F32)]
    pallas_call x0 -> x6, Pallas kernels: none -> 42.9 us  [the longest x1 19.2 us: backward(): pl.pallas_call(backward_kernel, grid=(groups,), in_specs=[tall, tall, tal...]
    while x10 -> x0, matrix products: 28.5 us -> none
    unnamed x27 -> x45, local copies, waits for them, and re-layouts: 33.6 us -> 12 us
    another operation x4 -> x0, loops' own time: 20.1 us -> none  [the longest x2 19.6 us: local_forward(): lax.scan(advance, start_state, (x_blocks, b_blocks, c_blocks, l_blocks))]
  transfers between devices with their start and end apart: 16 -> 25, of which waited for: 15 -> 13; matrix products, arithmetic and copies ran while one was open for 4% -> 6% of each run, Pallas kernels for 0% -> 17%
where the time goes in v1:
time: 209 us; the launch traced here: 208 us
  waiting for transfers between devices  92 us (44%)
  Pallas kernels  42.9 us (21%)
  starting transfers between devices  40 us (19%)
  local copies, waits for them, and re-layouts  14.1 us (7%)
  other arithmetic  11 us (5%)
  matrix products  7.03 us (3%)
    ppermute x14, waiting for transfers between devices, on_device(): lax.ppermute(part.astype(BF16), 'ctx', hops)  67.2 us
    ppermute x6, waiting for transfers between devices, scan_states(): enter = lax.ppermute(out.astype(BF16), 'ctx', pairs).astype(F32)  23.4 us
    pallas_call x1, Pallas kernels, backward(): pl.pallas_call(backward_kernel, grid=(groups,), in_specs=[tall, tall, tal...  19.2 us
    ppermute x14, starting transfers between devices, on_device(): lax.ppermute(part.astype(BF16), 'ctx', hops)  17.5 us
    ppermute x6, starting transfers between devices, scan_states(): enter = lax.ppermute(out.astype(BF16), 'ctx', pairs).astype(F32)  16.3 us
    unnamed x45, local copies, waits for them, and re-layouts  12 us
    pallas_call x1, Pallas kernels, forward(): pl.pallas_call(forward_kernel, grid=(groups,), in_specs=[pl.BlockSpec((ro...  7.88 us
    dot_general x16, matrix products, dot(): lax.dot_general(a, b, dims, precision=precision, preferred_element_type=F32)  7.03 us
  transfers between devices with their start and end apart: 25, of which 13 were waited for; matrix products, arithmetic and copies ran while one was open for 6% of the time, Pallas kernels for 17%

profile of v1, /device:TPU:0, one launch (start us, length us, event | category | flops | bytes accessed | tf_op | source)
XLA Modules:
  0.0 208.1 jit_solution(10968833484212519078)
XLA Ops:
  4.3 3.8 %start.1 = (f32[4,512,8]{2,1,0:T(8,128)S(1)}, f32[32,512]{1,0:T(8,128)S(1)}, f32[4,512,8]{2,1,0:T(8,128)S(1)}, bf16[144,1024]{1,0:T(8,128)(2,1)S(1)}, f32[128,1024]{1,0:T(8,128)S(1)}, /*index=5*/f32[8,1024]{1,0:T(8,128)S(1)}) custom-call(s32[1]{0:T(128)} %bitcast.q_ref, f32[512,32]{1,0:T(8,128)S(1)} %copy.14.loga_ref, bf16[512,2048]{1,0:T(8,128)(2,1)S(1)} %copy-done.6, ...), custom_call_target="tpu_custom_call" | custom-call | flops 1000000000 | bytes 6291456 | tf_op jit(solution)/shard_map/start/pallas_call | solution.py:108
  9.1 3.0 %collective-permute-start = (bf16[144,1024]{1,0:T(8,128)(2,1)S(1)}, bf16[144,1024]{1,0:T(8,128)(2,1)}, u32[]{:S(2)}, u32[]{:S(2)}) collective-permute-start(bf16[144,1024]{1,0:T(8,128)(2,1)S(1)} %get-tuple-element.22), channel_id=1, source_target_pairs={{0,2},{2,0},{4,6},{6,4},{8,10},{10,8},{12,14},{14,12},{1,3},{3,1},... | collective-permute-start | bytes 884744 | tf_op jit(solution)/shard_map/ppermute | solution.py:429
  12.1 3.4 %copy-done.5 = bf16[2048,2048]{1,0:T(8,128)(2,1)S(1)} copy-done((bf16[2048,2048]{1,0:T(8,128)(2,1)S(1)}, bf16[2048,2048]{1,0:T(8,128)(2,1)}, u32[]{:S(2)}) %copy-start.5) | copy-done | bytes 8388632
  15.5 6.9 %adjoint.1 = (bf16[512,2048]{1,0:T(8,128)(2,1)S(1)}, f32[128,2048]{1,0:T(8,128)S(1)}) custom-call(bf16[512,2048]{1,0:T(8,128)(2,1)S(1)} %copy-done.2, bf16[2048,2048]{1,0:T(8,128)(2,1)S(1)} %copy-done.5, bf16[512,128]{1,0:T(8,128)(2,1)S(1)} %copy-done.4, f32[4,512,8]{2,1,0:T(8,128)S(1)} %get-tuple-element.17.lead_ref), custom_call_target="tpu_custom_call" | custom-call | flops 6000000000 | bytes 14680064 | tf_op jit(solution)/shard_map/adjoint/pallas_call | solution.py:239
  24.6 1.8 fusion.86
  26.4 4.0 %collective-permute-start.1 = (bf16[128,1024]{1,0:T(8,128)(2,1)}, bf16[128,1024]{1,0:T(8,128)(2,1)S(1)}, u32[]{:S(2)}, u32[]{:S(2)}) collective-permute-start(bf16[128,1024]{1,0:T(8,128)(2,1)} %fusion.86), channel_id=1, source_target_pairs={{0,4},{2,6},{4,8},{6,10},{8,12},{10,14},{1,5},{3,7},{5,9},{7,11},{... | collective-permute-start | bytes 786440 | tf_op jit(solution)/shard_map/ppermute | solution.py:410
  31.6 4.0 %collective-permute-done.1 = bf16[128,1024]{1,0:T(8,128)(2,1)S(1)} collective-permute-done((bf16[128,1024]{1,0:T(8,128)(2,1)}, bf16[128,1024]{1,0:T(8,128)(2,1)S(1)}, u32[]{:S(2)}, u32[]{:S(2)}) %collective-permute-start.1) | collective-permute-done | bytes 262176 | tf_op jit(solution)/shard_map/ppermute | solution.py:410
  38.3 7.8 %collective-permute-done.6 = bf16[128,1024]{1,0:T(8,128)(2,1)S(1)} collective-permute-done((bf16[128,1024]{1,0:T(8,128)(2,1)S(1)}, bf16[128,1024]{1,0:T(8,128)(2,1)S(1)}, u32[]{:S(2)}, u32[]{:S(2)}) %collective-permute-start.6) | collective-permute-done | bytes 262176 | tf_op jit(solution)/shard_map/ppermute | solution.py:410
  47.4 4.6 %collective-permute-start.2 = (bf16[128,1024]{1,0:T(8,128)(2,1)S(1)}, bf16[128,1024]{1,0:T(8,128)(2,1)S(1)}, u32[]{:S(2)}, u32[]{:S(2)}) collective-permute-start(bf16[128,1024]{1,0:T(8,128)(2,1)S(1)} %get-tuple-element.40), channel_id=1, source_target_pairs={{0,4},{2,6},{4,8},{6,10},{8,12},{10,14},{1,5},{3,7},{5,9},{7,11},{... | collective-permute-start | bytes 786440 | tf_op jit(solution)/shard_map/ppermute | solution.py:410
  52.0 2.4 %collective-permute-done.7 = bf16[128,1024]{1,0:T(8,128)(2,1)S(1)} collective-permute-done((bf16[128,1024]{1,0:T(8,128)(2,1)S(1)}, bf16[128,1024]{1,0:T(8,128)(2,1)S(1)}, u32[]{:S(2)}, u32[]{:S(2)}) %collective-permute-start.7) | collective-permute-done | bytes 262176 | tf_op jit(solution)/shard_map/ppermute | solution.py:410
  56.1 7.0 %collective-permute-done.8 = bf16[128,1024]{1,0:T(8,128)(2,1)S(1)} collective-permute-done((bf16[128,1024]{1,0:T(8,128)(2,1)S(1)}, bf16[128,1024]{1,0:T(8,128)(2,1)S(1)}, u32[]{:S(2)}, u32[]{:S(2)}) %collective-permute-start.8) | collective-permute-done | bytes 262176 | tf_op jit(solution)/shard_map/ppermute | solution.py:410
  63.1 2.0 fusion.9
  65.1 3.6 %collective-permute-start.3 = (bf16[128,1024]{1,0:T(8,128)(2,1)S(1)}, bf16[128,1024]{1,0:T(8,128)(2,1)S(1)}, u32[]{:S(2)}, u32[]{:S(2)}) collective-permute-start(bf16[128,1024]{1,0:T(8,128)(2,1)S(1)} %get-tuple-element.44), channel_id=1, source_target_pairs={{0,4},{2,6},{4,8},{6,10},{8,12},{10,14},{1,5},{3,7},{5,9},{7,11},{... | collective-permute-start | bytes 786440 | tf_op jit(solution)/shard_map/ppermute | solution.py:410
  70.3 2.3 %collective-permute-done.3 = bf16[128,1024]{1,0:T(8,128)(2,1)S(1)} collective-permute-done((bf16[128,1024]{1,0:T(8,128)(2,1)S(1)}, bf16[128,1024]{1,0:T(8,128)(2,1)S(1)}, u32[]{:S(2)}, u32[]{:S(2)}) %collective-permute-start.3) | collective-permute-done | bytes 262176 | tf_op jit(solution)/shard_map/ppermute | solution.py:410
  75.0 7.9 %forward.1.y_ref = f32[512,2048]{1,0:T(8,128)S(1)} custom-call(bf16[512,2048]{1,0:T(8,128)(2,1)S(1)} %copy-done.7, bf16[512,128]{1,0:T(8,128)(2,1)S(1)} %copy-done.10, bf16[512,128]{1,0:T(8,128)(2,1)S(1)} %copy-done.4, f32[4,512,8]{2,1,0:T(8,128)S(1)} %copy-done.12, f32[32,512]{1,0:T(8,128)S(1)} %get-tuple-element.20.cumt_ref), custom_call_target="tpu_custom_call" | custom-call | flops 6000000000 | bytes 7340032 | tf_op jit(solution)/shard_map/forward/pallas_call | solution.py:176
  82.9 2.0 copy-done
  86.8 2.0 turn.1
  91.4 3.0 %finish.1.y_ref = bf16[512,2048]{1,0:T(8,128)(2,1)S(1)} custom-call(f32[512,2048]{1,0:T(8,128)S(1)} %copy-done.1, bf16[512,128]{1,0:T(8,128)(2,1)S(1)} %copy-done.4, f32[4,512,8]{2,1,0:T(8,128)S(1)} %get-tuple-element.17.lead_ref, bf16[128,2048]{1,0:T(8,128)(2,1)S(1)} %get-tuple-element.45.state_ref.s_ref), custom_call_target="tpu_custom_call" | custom-call | flops 300000000 | bytes 7340032 | tf_op jit(solution)/shard_map/finish/pallas_call | solution.py:206
  94.8 2.5 %collective-permute-start.11 = (bf16[256,1024]{1,0:T(8,128)(2,1)S(1)}, bf16[256,1024]{1,0:T(8,128)(2,1)S(1)}, u32[]{:S(2)}, u32[]{:S(2)}) collective-permute-start(bf16[256,1024]{1,0:T(8,128)(2,1)S(1)} %convolution_convert_fusion.1), channel_id=1, source_target_pairs={{0,4},{4,8},{8,12},{12,14},{14,10},{10,6},{6,2},{2,0},{1,5},{5,9},... | collective-permute-start | bytes 1572872 | tf_op jit(solution)/shard_map/ppermute | solution.py:464
  97.9 10.3 %collective-permute-done.11 = bf16[256,1024]{1,0:T(8,128)(2,1)S(1)} collective-permute-done((bf16[256,1024]{1,0:T(8,128)(2,1)S(1)}, bf16[256,1024]{1,0:T(8,128)(2,1)S(1)}, u32[]{:S(2)}, u32[]{:S(2)}) %collective-permute-start.11) | collective-permute-done | bytes 524320 | tf_op jit(solution)/shard_map/ppermute | solution.py:464
  108.7 2.7 %collective-permute-start.12 = (bf16[256,1024]{1,0:T(8,128)(2,1)S(1)}, bf16[256,1024]{1,0:T(8,128)(2,1)S(1)}, u32[]{:S(2)}, u32[]{:S(2)}) collective-permute-start(bf16[256,1024]{1,0:T(8,128)(2,1)S(1)} %add_convert_fusion.11), channel_id=1, source_target_pairs={{0,4},{4,8},{8,12},{12,14},{14,10},{10,6},{6,2},{2,0},{1,5},{5,9},... | collective-permute-start | bytes 1572872 | tf_op jit(solution)/shard_map/ppermute | solution.py:464
  111.9 11.4 %collective-permute-done.12 = bf16[256,1024]{1,0:T(8,128)(2,1)S(1)} collective-permute-done((bf16[256,1024]{1,0:T(8,128)(2,1)S(1)}, bf16[256,1024]{1,0:T(8,128)(2,1)S(1)}, u32[]{:S(2)}, u32[]{:S(2)}) %collective-permute-start.12) | collective-permute-done | bytes 524320 | tf_op jit(solution)/shard_map/ppermute | solution.py:464
  123.8 2.5 %collective-permute-start.13 = (bf16[256,1024]{1,0:T(8,128)(2,1)S(1)}, bf16[256,1024]{1,0:T(8,128)(2,1)S(1)}, u32[]{:S(2)}, u32[]{:S(2)}) collective-permute-start(bf16[256,1024]{1,0:T(8,128)(2,1)S(1)} %add_convert_fusion.10), channel_id=1, source_target_pairs={{0,4},{4,8},{8,12},{12,14},{14,10},{10,6},{6,2},{2,0},{1,5},{5,9},... | collective-permute-start | bytes 1572872 | tf_op jit(solution)/shard_map/ppermute | solution.py:464
  126.8 11.3 %collective-permute-done.13 = bf16[256,1024]{1,0:T(8,128)(2,1)S(1)} collective-permute-done((bf16[256,1024]{1,0:T(8,128)(2,1)S(1)}, bf16[256,1024]{1,0:T(8,128)(2,1)S(1)}, u32[]{:S(2)}, u32[]{:S(2)}) %collective-permute-start.13) | collective-permute-done | bytes 524320 | tf_op jit(solution)/shard_map/ppermute | solution.py:464
  138.6 2.5 %collective-permute-start.14 = (bf16[256,1024]{1,0:T(8,128)(2,1)S(1)}, bf16[256,1024]{1,0:T(8,128)(2,1)S(1)}, u32[]{:S(2)}, u32[]{:S(2)}) collective-permute-start(bf16[256,1024]{1,0:T(8,128)(2,1)S(1)} %add_convert_fusion.9), channel_id=1, source_target_pairs={{0,4},{4,8},{8,12},{12,14},{14,10},{10,6},{6,2},{2,0},{1,5},{5,9},... | collective-permute-start | bytes 1572872 | tf_op jit(solution)/shard_map/ppermute | solution.py:464
  141.7 10.5 %collective-permute-done.14 = bf16[256,1024]{1,0:T(8,128)(2,1)S(1)} collective-permute-done((bf16[256,1024]{1,0:T(8,128)(2,1)S(1)}, bf16[256,1024]{1,0:T(8,128)(2,1)S(1)}, u32[]{:S(2)}, u32[]{:S(2)}) %collective-permute-start.14) | collective-permute-done | bytes 524320 | tf_op jit(solution)/shard_map/ppermute | solution.py:464
  152.6 2.5 %collective-permute-start.15 = (bf16[256,1024]{1,0:T(8,128)(2,1)S(1)}, bf16[256,1024]{1,0:T(8,128)(2,1)S(1)}, u32[]{:S(2)}, u32[]{:S(2)}) collective-permute-start(bf16[256,1024]{1,0:T(8,128)(2,1)S(1)} %add_convert_fusion.8), channel_id=1, source_target_pairs={{0,4},{4,8},{8,12},{12,14},{14,10},{10,6},{6,2},{2,0},{1,5},{5,9},... | collective-permute-start | bytes 1572872 | tf_op jit(solution)/shard_map/ppermute | solution.py:464
  155.7 19.2 %backward.1 = (bf16[512,2048]{1,0:T(8,128)(2,1)}, f32[512,128]{1,0:T(8,128)S(1)}, f32[512,128]{1,0:T(8,128)S(1)}, f32[32,512]{1,0:T(8,128)}) custom-call(bf16[512,2048]{1,0:T(8,128)(2,1)S(1)} %copy-done.8, bf16[512,2048]{1,0:T(8,128)(2,1)S(1)} %copy-done.15, bf16[512,2048]{1,0:T(8,128)(2,1)S(1)} %finish.1.y_ref, bf16[512,128]{1,0:T(8,128)(2,1)S(1)} %copy-done.10, ...), custom_call_target="tpu_custom_call" | custom-call | flops 10000000000 | bytes 10485760 | tf_op jit(solution)/shard_map/backward/pallas_call | solution.py:371
  175.6 2.0 collective-permute-start.16
  178.2 11.7 %collective-permute-done.16 = bf16[256,1024]{1,0:T(8,128)(2,1)S(1)} collective-permute-done((bf16[256,1024]{1,0:T(8,128)(2,1)S(1)}, bf16[256,1024]{1,0:T(8,128)(2,1)S(1)}, u32[]{:S(2)}, u32[]{:S(2)}) %collective-permute-start.16) | collective-permute-done | bytes 524320 | tf_op jit(solution)/shard_map/ppermute | solution.py:464
  190.4 2.0 collective-permute-start.17
  193.8 10.2 %collective-permute-done.17 = bf16[256,1024]{1,0:T(8,128)(2,1)S(1)} collective-permute-done((bf16[256,1024]{1,0:T(8,128)(2,1)S(1)}, bf16[256,1024]{1,0:T(8,128)(2,1)S(1)}, u32[]{:S(2)}, u32[]{:S(2)}) %collective-permute-start.17) | collective-permute-done | bytes 524320 | tf_op jit(solution)/shard_map/ppermute | solution.py:464
  (107 shorter events, 34.0 us)
Async XLA Ops:
  9.1 14.7 %collective-permute-start = (bf16[144,1024]{1,0:T(8,128)(2,1)S(1)}, bf16[144,1024]{1,0:T(8,128)(2,1)}, u32[]{:S(2)}, u32[]{:S(2)}) collective-permute-start(bf16[144,1024]{1,0:T(8,128)(2,1)S(1)} %get-tuple-element.22), channel_id=1, source_target_pairs={{0,2},{2,0},{4,6},{6,4},{8,10},{10,8},{12,14},{14,12},{1,3},{3,1},... | collective-permute-start | bytes 884744 | tf_op jit(solution)/shard_map/ppermute | solution.py:429
  23.7 7.9 %collective-permute-start.5 = (bf16[128,1024]{1,0:T(8,128)(2,1)S(1)}, bf16[128,1024]{1,0:T(8,128)(2,1)}, u32[]{:S(2)}, u32[]{:S(2)}) collective-permute-start(bf16[128,1024]{1,0:T(8,128)(2,1)S(1)} %select_convert_fusion), channel_id=1, source_target_pairs={{0,2},{2,0},{4,6},{6,4},{8,10},{10,8},{12,14},{14,12},{1,3},{3,1},... | collective-permute-start | bytes 786440 | tf_op jit(solution)/shard_map/ppermute | solution.py:440
  26.4 9.3 %collective-permute-start.1 = (bf16[128,1024]{1,0:T(8,128)(2,1)}, bf16[128,1024]{1,0:T(8,128)(2,1)S(1)}, u32[]{:S(2)}, u32[]{:S(2)}) collective-permute-start(bf16[128,1024]{1,0:T(8,128)(2,1)} %fusion.86), channel_id=1, source_target_pairs={{0,4},{2,6},{4,8},{6,10},{8,12},{10,14},{1,5},{3,7},{5,9},{7,11},{... | collective-permute-start | bytes 786440 | tf_op jit(solution)/shard_map/ppermute | solution.py:410
  37.0 9.1 %collective-permute-start.6 = (bf16[128,1024]{1,0:T(8,128)(2,1)S(1)}, bf16[128,1024]{1,0:T(8,128)(2,1)S(1)}, u32[]{:S(2)}, u32[]{:S(2)}) collective-permute-start(bf16[128,1024]{1,0:T(8,128)(2,1)S(1)} %get-tuple-element.29), channel_id=1, source_target_pairs={{4,0},{6,2},{8,4},{10,6},{12,8},{14,10},{5,1},{7,3},{9,5},{11,7},{... | collective-permute-start | bytes 786440 | tf_op jit(solution)/shard_map/ppermute | solution.py:410
  46.1 8.3 %collective-permute-start.7 = (bf16[128,1024]{1,0:T(8,128)(2,1)S(1)}, bf16[128,1024]{1,0:T(8,128)(2,1)S(1)}, u32[]{:S(2)}, u32[]{:S(2)}) collective-permute-start(bf16[128,1024]{1,0:T(8,128)(2,1)S(1)} %add_convert_fusion.13), channel_id=1, source_target_pairs={{4,0},{6,2},{8,4},{10,6},{12,8},{14,10},{5,1},{7,3},{9,5},{11,7},{... | collective-permute-start | bytes 786440 | tf_op jit(solution)/shard_map/ppermute | solution.py:410
  47.4 8.7 %collective-permute-start.2 = (bf16[128,1024]{1,0:T(8,128)(2,1)S(1)}, bf16[128,1024]{1,0:T(8,128)(2,1)S(1)}, u32[]{:S(2)}, u32[]{:S(2)}) collective-permute-start(bf16[128,1024]{1,0:T(8,128)(2,1)S(1)} %get-tuple-element.40), channel_id=1, source_target_pairs={{0,4},{2,6},{4,8},{6,10},{8,12},{10,14},{1,5},{3,7},{5,9},{7,11},{... | collective-permute-start | bytes 786440 | tf_op jit(solution)/shard_map/ppermute | solution.py:410
  54.5 20.4 %copy-start.7 = (bf16[512,2048]{1,0:T(8,128)(2,1)S(1)}, bf16[512,2048]{1,0:T(8,128)(2,1)}, u32[]{:S(2)}) copy-start(bf16[512,2048]{1,0:T(8,128)(2,1)} %x_ref.5) | copy-start | bytes 6291460
  54.5 20.4 %copy-start.10 = (bf16[512,128]{1,0:T(8,128)(2,1)S(1)}, bf16[512,128]{1,0:T(8,128)(2,1)}, u32[]{:S(2)}) copy-start(bf16[512,128]{1,0:T(8,128)(2,1)} %b_ref.5) | copy-start | bytes 393220
  54.5 20.4 %copy-start.12 = (f32[4,512,8]{2,1,0:T(8,128)S(1)}, f32[4,512,8]{2,1,0:T(8,128)}, u32[]{:S(2)}) copy-start(f32[4,512,8]{2,1,0:T(8,128)} %copy-done.11) | copy-start | bytes 196612
  54.5 8.5 %collective-permute-start.8 = (bf16[128,1024]{1,0:T(8,128)(2,1)S(1)}, bf16[128,1024]{1,0:T(8,128)(2,1)S(1)}, u32[]{:S(2)}, u32[]{:S(2)}) collective-permute-start(bf16[128,1024]{1,0:T(8,128)(2,1)S(1)} %add_convert_fusion.12), channel_id=1, source_target_pairs={{4,0},{6,2},{8,4},{10,6},{12,8},{14,10},{5,1},{7,3},{9,5},{11,7},{... | collective-permute-start | bytes 786440 | tf_op jit(solution)/shard_map/ppermute | solution.py:410
  63.1 11.9 %copy-start.19 = (bf16[128,1024]{1,0:T(8,128)(2,1)}, bf16[128,1024]{1,0:T(8,128)(2,1)S(1)}, u32[]{:S(2)}) copy-start(bf16[128,1024]{1,0:T(8,128)(2,1)S(1)} %collective-permute-done.8) | copy-start | bytes 786436
  65.1 7.5 %collective-permute-start.3 = (bf16[128,1024]{1,0:T(8,128)(2,1)S(1)}, bf16[128,1024]{1,0:T(8,128)(2,1)S(1)}, u32[]{:S(2)}, u32[]{:S(2)}) collective-permute-start(bf16[128,1024]{1,0:T(8,128)(2,1)S(1)} %get-tuple-element.44), channel_id=1, source_target_pairs={{0,4},{2,6},{4,8},{6,10},{8,12},{10,14},{1,5},{3,7},{5,9},{7,11},{... | collective-permute-start | bytes 786440 | tf_op jit(solution)/shard_map/ppermute | solution.py:410
  68.8 20.1 %collective-permute-start.9 = (bf16[128,1024]{1,0:T(8,128)(2,1)}, bf16[128,1024]{1,0:T(8,128)(2,1)}, u32[]{:S(2)}, u32[]{:S(2)}) collective-permute-start(bf16[128,1024]{1,0:T(8,128)(2,1)} %get-tuple-element.43), channel_id=1, source_target_pairs={{0,2},{2,0},{4,6},{6,4},{8,10},{10,8},{12,14},{14,12},{1,3},{3,1},... | collective-permute-start | bytes 786440 | tf_op jit(solution)/shard_map/ppermute | solution.py:442
  73.4 15.5 %collective-permute-start.4 = (bf16[128,1024]{1,0:T(8,128)(2,1)}, bf16[128,1024]{1,0:T(8,128)(2,1)}, u32[]{:S(2)}, u32[]{:S(2)}) collective-permute-start(bf16[128,1024]{1,0:T(8,128)(2,1)} %fusion.6), channel_id=1, source_target_pairs={{0,2},{2,0},{4,6},{6,4},{8,10},{10,8},{12,14},{14,12},{1,3},{3,1},... | collective-permute-start | bytes 786440 | tf_op jit(solution)/shard_map/ppermute | solution.py:433
  94.8 13.4 %collective-permute-start.11 = (bf16[256,1024]{1,0:T(8,128)(2,1)S(1)}, bf16[256,1024]{1,0:T(8,128)(2,1)S(1)}, u32[]{:S(2)}, u32[]{:S(2)}) collective-permute-start(bf16[256,1024]{1,0:T(8,128)(2,1)S(1)} %convolution_convert_fusion.1), channel_id=1, source_target_pairs={{0,4},{4,8},{8,12},{12,14},{14,10},{10,6},{6,2},{2,0},{1,5},{5,9},... | collective-permute-start | bytes 1572872 | tf_op jit(solution)/shard_map/ppermute | solution.py:464
  97.8 13.6 %collective-permute-start.18 = (bf16[256,1024]{1,0:T(8,128)(2,1)S(1)}, bf16[256,1024]{1,0:T(8,128)(2,1)S(1)}, u32[]{:S(2)}, u32[]{:S(2)}) collective-permute-start(bf16[256,1024]{1,0:T(8,128)(2,1)S(1)} %convolution_convert_fusion), channel_id=1, source_target_pairs={{0,2},{4,0},{8,4},{12,8},{14,12},{10,14},{6,10},{2,6},{1,3},{5,1},... | collective-permute-start | bytes 1572872 | tf_op jit(solution)/shard_map/ppermute | solution.py:464
  108.7 14.6 %collective-permute-start.12 = (bf16[256,1024]{1,0:T(8,128)(2,1)S(1)}, bf16[256,1024]{1,0:T(8,128)(2,1)S(1)}, u32[]{:S(2)}, u32[]{:S(2)}) collective-permute-start(bf16[256,1024]{1,0:T(8,128)(2,1)S(1)} %add_convert_fusion.11), channel_id=1, source_target_pairs={{0,4},{4,8},{8,12},{12,14},{14,10},{10,6},{6,2},{2,0},{1,5},{5,9},... | collective-permute-start | bytes 1572872 | tf_op jit(solution)/shard_map/ppermute | solution.py:464
  111.8 14.5 %collective-permute-start.19 = (bf16[256,1024]{1,0:T(8,128)(2,1)S(1)}, bf16[256,1024]{1,0:T(8,128)(2,1)S(1)}, u32[]{:S(2)}, u32[]{:S(2)}) collective-permute-start(bf16[256,1024]{1,0:T(8,128)(2,1)S(1)} %add_convert_fusion.5), channel_id=1, source_target_pairs={{0,2},{4,0},{8,4},{12,8},{14,12},{10,14},{6,10},{2,6},{1,3},{5,1},... | collective-permute-start | bytes 1572872 | tf_op jit(solution)/shard_map/ppermute | solution.py:464
  123.8 14.4 %collective-permute-start.13 = (bf16[256,1024]{1,0:T(8,128)(2,1)S(1)}, bf16[256,1024]{1,0:T(8,128)(2,1)S(1)}, u32[]{:S(2)}, u32[]{:S(2)}) collective-permute-start(bf16[256,1024]{1,0:T(8,128)(2,1)S(1)} %add_convert_fusion.10), channel_id=1, source_target_pairs={{0,4},{4,8},{8,12},{12,14},{14,10},{10,6},{6,2},{2,0},{1,5},{5,9},... | collective-permute-start | bytes 1572872 | tf_op jit(solution)/shard_map/ppermute | solution.py:464
  126.8 14.4 %collective-permute-start.20 = (bf16[256,1024]{1,0:T(8,128)(2,1)S(1)}, bf16[256,1024]{1,0:T(8,128)(2,1)S(1)}, u32[]{:S(2)}, u32[]{:S(2)}) collective-permute-start(bf16[256,1024]{1,0:T(8,128)(2,1)S(1)} %add_convert_fusion.4), channel_id=1, source_target_pairs={{0,2},{4,0},{8,4},{12,8},{14,12},{10,14},{6,10},{2,6},{1,3},{5,1},... | collective-permute-start | bytes 1572872 | tf_op jit(solution)/shard_map/ppermute | solution.py:464
  138.6 13.6 %collective-permute-start.14 = (bf16[256,1024]{1,0:T(8,128)(2,1)S(1)}, bf16[256,1024]{1,0:T(8,128)(2,1)S(1)}, u32[]{:S(2)}, u32[]{:S(2)}) collective-permute-start(bf16[256,1024]{1,0:T(8,128)(2,1)S(1)} %add_convert_fusion.9), channel_id=1, source_target_pairs={{0,4},{4,8},{8,12},{12,14},{14,10},{10,6},{6,2},{2,0},{1,5},{5,9},... | collective-permute-start | bytes 1572872 | tf_op jit(solution)/shard_map/ppermute | solution.py:464
  141.6 14.2 %copy-start.8 = (bf16[512,2048]{1,0:T(8,128)(2,1)S(1)}, bf16[512,2048]{1,0:T(8,128)(2,1)}, u32[]{:S(2)}) copy-start(bf16[512,2048]{1,0:T(8,128)(2,1)} %x_ref.5) | copy-start | bytes 6291460
  141.6 14.1 %copy-start.13 = (f32[4,512,8]{2,1,0:T(8,128)S(1)}, f32[4,512,8]{2,1,0:T(8,128)}, u32[]{:S(2)}) copy-start(f32[4,512,8]{2,1,0:T(8,128)} %copy-done.11) | copy-start | bytes 196612
  141.6 14.1 %copy-start.15 = (bf16[512,2048]{1,0:T(8,128)(2,1)S(1)}, bf16[512,2048]{1,0:T(8,128)(2,1)}, u32[]{:S(2)}) copy-start(bf16[512,2048]{1,0:T(8,128)(2,1)} %copy-done.14) | copy-start | bytes 6291460
  141.6 13.6 %collective-permute-start.21 = (bf16[256,1024]{1,0:T(8,128)(2,1)S(1)}, bf16[256,1024]{1,0:T(8,128)(2,1)S(1)}, u32[]{:S(2)}, u32[]{:S(2)}) collective-permute-start(bf16[256,1024]{1,0:T(8,128)(2,1)S(1)} %add_convert_fusion.3), channel_id=1, source_target_pairs={{0,2},{4,0},{8,4},{12,8},{14,12},{10,14},{6,10},{2,6},{1,3},{5,1},... | collective-permute-start | bytes 1572872 | tf_op jit(solution)/shard_map/ppermute | solution.py:464
  152.6 22.5 %collective-permute-start.15 = (bf16[256,1024]{1,0:T(8,128)(2,1)S(1)}, bf16[256,1024]{1,0:T(8,128)(2,1)S(1)}, u32[]{:S(2)}, u32[]{:S(2)}) collective-permute-start(bf16[256,1024]{1,0:T(8,128)(2,1)S(1)} %add_convert_fusion.8), channel_id=1, source_target_pairs={{0,4},{4,8},{8,12},{12,14},{14,10},{10,6},{6,2},{2,0},{1,5},{5,9},... | collective-permute-start | bytes 1572872 | tf_op jit(solution)/shard_map/ppermute | solution.py:464
  155.6 22.0 %collective-permute-start.22 = (bf16[256,1024]{1,0:T(8,128)(2,1)S(1)}, bf16[256,1024]{1,0:T(8,128)(2,1)S(1)}, u32[]{:S(2)}, u32[]{:S(2)}) collective-permute-start(bf16[256,1024]{1,0:T(8,128)(2,1)S(1)} %add_convert_fusion.2), channel_id=1, source_target_pairs={{0,2},{4,0},{8,4},{12,8},{14,12},{10,14},{6,10},{2,6},{1,3},{5,1},... | collective-permute-start | bytes 1572872 | tf_op jit(solution)/shard_map/ppermute | solution.py:464
  175.0 3.1 %collective-permute-start.10 = (bf16[1024,128]{1,0:T(8,128)(2,1)S(1)}, bf16[1024,128]{1,0:T(8,128)(2,1)S(1)}, u32[]{:S(2)}, u32[]{:S(2)}) collective-permute-start(bf16[1024,128]{1,0:T(8,128)(2,1)S(1)} %pad_maximum_fusion.3), channel_id=1, source_target_pairs={{0,1},{1,0},{2,3},{3,2},{4,5},{5,4},{6,7},{7,6},{8,9},{9,8},{10,11... | collective-permute-start | bytes 786440 | tf_op jit(solution)/shard_map/ppermute | solution.py:469
  175.6 14.4 %collective-permute-start.16 = (bf16[256,1024]{1,0:T(8,128)(2,1)S(1)}, bf16[256,1024]{1,0:T(8,128)(2,1)S(1)}, u32[]{:S(2)}, u32[]{:S(2)}) collective-permute-start(bf16[256,1024]{1,0:T(8,128)(2,1)S(1)} %add_convert_fusion.7), channel_id=1, source_target_pairs={{0,4},{4,8},{8,12},{12,14},{14,10},{10,6},{6,2},{2,0},{1,5},{5,9},... | collective-permute-start | bytes 1572872 | tf_op jit(solution)/shard_map/ppermute | solution.py:464
  178.0 14.4 %collective-permute-start.23 = (bf16[256,1024]{1,0:T(8,128)(2,1)S(1)}, bf16[256,1024]{1,0:T(8,128)(2,1)S(1)}, u32[]{:S(2)}, u32[]{:S(2)}) collective-permute-start(bf16[256,1024]{1,0:T(8,128)(2,1)S(1)} %add_convert_fusion.1), channel_id=1, source_target_pairs={{0,2},{4,0},{8,4},{12,8},{14,12},{10,14},{6,10},{2,6},{1,3},{5,1},... | collective-permute-start | bytes 1572872 | tf_op jit(solution)/shard_map/ppermute | solution.py:464
  190.4 13.6 %collective-permute-start.17 = (bf16[256,1024]{1,0:T(8,128)(2,1)S(1)}, bf16[256,1024]{1,0:T(8,128)(2,1)S(1)}, u32[]{:S(2)}, u32[]{:S(2)}) collective-permute-start(bf16[256,1024]{1,0:T(8,128)(2,1)S(1)} %add_convert_fusion.6), channel_id=1, source_target_pairs={{0,4},{4,8},{8,12},{12,14},{14,10},{10,6},{6,2},{2,0},{1,5},{5,9},... | collective-permute-start | bytes 1572872 | tf_op jit(solution)/shard_map/ppermute | solution.py:464
  192.9 13.3 %collective-permute-start.24 = (bf16[256,1024]{1,0:T(8,128)(2,1)S(1)}, bf16[256,1024]{1,0:T(8,128)(2,1)S(1)}, u32[]{:S(2)}, u32[]{:S(2)}) collective-permute-start(bf16[256,1024]{1,0:T(8,128)(2,1)S(1)} %add_convert_fusion), channel_id=1, source_target_pairs={{0,2},{4,0},{8,4},{12,8},{14,12},{10,14},{6,10},{2,6},{1,3},{5,1},... | collective-permute-start | bytes 1572872 | tf_op jit(solution)/shard_map/ppermute | solution.py:464
  (15 other events, 74.1 us)
